TPU v7x, 32 devices: a whole 2x2x4 slice. The times are simulated.
32 devices in a mesh: groups: 2 (over y), down: 4 (over z), cross: 2 (over x), depth: 2 (over core).
Axes of the slice: x: 2, y: 2, z: 4, core: 2. Of those that a mesh axis runs over, the one named last changes fastest.
Arguments:
- positions: float32 [3, 16, 4, 4, 128], P(None, ('groups', 'down'), 'cross', 'depth'), parts along dimension 1, may hold values from -0.5 to 0.5
- velocities: float32 [3, 16, 4, 4, 128], P(None, ('groups', 'down'), 'cross', 'depth'), parts along dimension 1, may hold values from -6 to 6
- sphere_radii: float32 [16, 4, 4, 128], P(('groups', 'down'), 'cross', 'depth'), parts along dimension 0, may hold values from 0.08 to 0.12
- counts: int32 [16, 4, 4], P(('groups', 'down'), 'cross', 'depth'), parts along dimension 0, may hold values from 32 to 128, as said below
- coefficients: float32 [48], replicated, may hold values from -0.6 to 0.6
Outputs:
- velocity_new: float32 [3, 16, 4, 4, 128], P(None, ('groups', 'down'), 'cross', 'depth'), parts along dimension 1
- contact_force: float32 [3, 16, 4, 4, 128], P(None, ('groups', 'down'), 'cross', 'depth'), parts along dimension 1
- residual_field: float32 [16, 4, 4], P(('groups', 'down'), 'cross', 'depth'), parts along dimension 0
- gram_matrix: float32 [96, 48], P('groups'), parts along dimension 0
- moment_vector: float32 [96], P('groups'), parts along dimension 0
There are 2 independent parts, one for each index of `groups`. A program takes and returns all parts, laid end to end along the dimension named above; an argument that names none is the same for every part. Nothing has to cross between parts.
Inputs may be any that keep to these rules, and one draw needn't show every extreme that they name: `counts`: slots 0 to count - 1 of a cell hold spheres, the rest are padding; every cell of the bottom depth layer holds 128.
All inputs are finite; a program needn't handle non-finite values.
Results may differ from a plain program's by a relative error of at most 0.0003.
Values sent between devices are 32-bit elements; how exact they have to be, the bound alone decides.
No kernel may reach another device: no remote copies, remote signals or barrier semaphores. Data moves between devices by JAX's collectives and lax.ppermute only.
A program may use at most 128 MiB of HBM per device.

v0:
```python
import functools

import jax
import jax.numpy as jnp
from jax import lax
from jax.experimental import pallas as pl
from jax.experimental.pallas import tpu as pltpu
from jax.sharding import PartitionSpec as P

STIFFNESS = 100.0
DAMPING = 20.0
TIME_STEP = 0.05
KERNEL_WIDTH = 0.4
KERNEL_NORM = 64.0
SOFTENING = 0.0001
RADIUS_REF = 0.1
MASS_SHIFT = 0.1
DEAD = -1000.0
TERMS = 48
S = 128
SPREAD = 4
F32 = jnp.float32
BF16 = jnp.bfloat16
CELLS = tuple((a, b, z) for a in range(2) for b in range(2) for z in range(2))
PAIR_LIST = ((0, 0), (0, 1), (0, 2), (1, 1), (1, 2), (2, 2))
VMEM_SPEC = pl.BlockSpec(memory_space=pltpu.VMEM)
SMEM_SPEC = pl.BlockSpec(memory_space=pltpu.SMEM)
VMEM_LIMIT = 48 * 1024 * 1024


def row_ids(shape):
    return lax.broadcasted_iota(jnp.int32, shape, 0)


def lane_ids(shape):
    return lax.broadcasted_iota(jnp.int32, shape, 1)


def one_hot(condition):
    return jnp.where(condition, 1.0, 0.0).astype(BF16)


def split(value):
    high = value.astype(BF16)
    return high, value - high.astype(F32)


def matmul(left, right):
    return lax.dot_general(left, right, (((1,), (0,)), ((), ())), preferred_element_type=F32)


def matmul_turned(left, right):
    return lax.dot_general(left, right, (((1,), (1,)), ((), ())), preferred_element_type=F32)


def lane_gather(table, index):
    return jnp.take_along_axis(table, index, axis=1)


def pack_kernel(
    counts_hbm, positions_hbm, velocities_hbm, radii_hbm, own, inner, counts, positions, velocities, radii, arrived
):
    copies = [
        pltpu.make_async_copy(source, target, arrived.at[k])
        for k, (source, target) in enumerate(
            (
                (counts_hbm, counts),
                (positions_hbm, positions),
                (velocities_hbm, velocities),
                (radii_hbm, radii),
            )
        )
    ]
    for copy in copies:
        copy.start()
    for copy in copies:
        copy.wait()
    depth = lax.axis_index("depth")
    lanes = lane_ids((1, S))

    def layer(ref, at, z):
        rows = ref[at]
        return jnp.where(depth == z, rows[0:1], rows[1:2])

    for c, (a, b, z) in enumerate(CELLS):
        for k in range(3):
            own[c * 8 + k : c * 8 + k + 1, :] = layer(positions, (k, a, b), z)
            own[c * 8 + 3 + k : c * 8 + 4 + k, :] = layer(velocities, (k, a, b), z)
        count = jnp.where(depth == z, counts[a, b, 0], counts[a, b, 1])
        own[c * 8 + 6 : c * 8 + 7, :] = jnp.where(lanes < count, layer(radii, (a, b), z), DEAD)
        own[c * 8 + 7 : c * 8 + 8, :] = jnp.zeros((1, S), F32)
    for column in range(4):
        inner[column * 8 : column * 8 + 8, :] = own[column * 16 + 8 : column * 16 + 16, :]


def local_state(raw, centre):
    rows = row_ids(raw.shape)
    shift = jnp.where(rows == 0, centre[0], jnp.where(rows == 1, centre[1], centre[2]))
    return jnp.where(rows < 3, raw + shift, jnp.where(rows < 6, DAMPING * raw, raw))


def plane_reader(refs, height):
    own, depth_halo, sides = refs[0], refs[1], refs[2:]

    def read(ref, cell):
        return ref[cell * height : cell * height + height, :]

    def cell(x, y, slot):
        a = x - 1
        if y in (1, 2):
            return read(own, a * 4 + (y - 1) * 2 + slot) if slot < 2 else read(depth_halo, a * 2 + y - 1)
        if len(sides) == 4:
            before, after, diag_before, diag_after = sides
            if slot < 2:
                return read(before if y == 0 else after, a * 2 + slot)
            return read(diag_before if y == 0 else diag_after, a)
        b = 1 if y == 0 else 0
        if slot < 2:
            return read(sides[0], a * 4 + b * 2 + slot)
        return read(sides[0], 8 + a * 2 + b) if len(sides) == 1 else read(sides[1], a * 2 + b)

    return cell


def down_reader(refs, height):
    even = lax.rem(lax.axis_index("down"), 2) == 0
    swapped = lax.axis_size("down") % 2 == 0

    def cell(x, y, slot):
        if y in (1, 2):
            place = (y - 1) * 2 + slot if slot < 2 else 4 + y - 1
        else:
            side = 0 if y == 0 else 1
            place = 6 + side * 2 + slot if slot < 2 else 10 + side
        one, two = (ref[place * height : place * height + height, :] for ref in refs)
        if swapped:
            return jnp.where(even, one, two) if x == 0 else jnp.where(even, two, one)
        return one if x == 0 else two

    return cell


def centre_of(x, y, slot, depth):
    side = 0.5 - depth.astype(F32)
    return (x - 1.5, y - 1.5, (-1.0, 1.0, 3.0)[slot] * side)


BLOCK = tuple((x, y, slot) for x in (1, 2) for y in (1, 2) for slot in (0, 1))
PLANE = tuple(
    (x, y, slot) for x in (1, 2) for y in range(4) for slot in range(3) if (x, y, slot) not in BLOCK
)
INSIDE = tuple((x, y, slot) for x in (1, 2) for y in range(4) for slot in range(3))
OUTSIDE = tuple((x, y, slot) for x in (0, 3) for y in range(4) for slot in range(3))


def stepped_state(old, speed, centre):
    rows = row_ids((3, S))
    shift = jnp.where(rows == 0, centre[0], jnp.where(rows == 1, centre[1], centre[2]))
    return (old[0:3] + TIME_STEP * speed[0:3]) + shift, DAMPING * speed[0:3], old[6:8]


def contact_scratch(cells, width):
    rows = len(cells)
    return [
        pltpu.VMEM((rows * 8, S), F32),
        pltpu.VMEM((8 * 8, S), F32),
        pltpu.VMEM((8 * rows, S), jnp.int32),
        pltpu.VMEM((8 * rows, S), jnp.int32),
        pltpu.VMEM((8 * rows, S), jnp.int32),
        pltpu.VMEM((8 * rows, S), jnp.int32),
        pltpu.VMEM((18 * 8 * S, 32), F32),
        pltpu.VMEM((width * 8 * 8, S), F32),
    ]


def store_listed(list_ref, t, c, chunk, tile):
    high = tile.astype(BF16).astype(F32)
    rest = tile - high
    middle = rest.astype(BF16).astype(F32)
    turned = jnp.transpose(jnp.concatenate([high, middle, rest - middle, tile], axis=0))
    for part in range(S // chunk):
        start = pl.multiple_of(t * (8 * S) + (part * 8 + c) * chunk, chunk)
        list_ref[pl.ds(start, chunk), :] = turned[part * chunk : (part + 1) * chunk]


def pair_step(width, chunk, mine_ref, list_ref, sum_ref):
    selector = jnp.logical_and(
        row_ids((32, SPREAD * S)) % 8 == lane_ids((32, SPREAD * S)) // S, row_ids((32, SPREAD * S)) < 24
    )
    selector = one_hot(selector)

    def one_step(step, carry):
        every = list_ref[pl.ds(pl.multiple_of(step * (8 * chunk), 8 * chunk), 8 * chunk), :]
        spread = matmul(every.astype(BF16), selector)
        for c in range(8):
            listed = every[c * chunk : (c + 1) * chunk]
            me = [jnp.broadcast_to(mine_ref[c * 8 + k : c * 8 + k + 1, :], (8, S)) for k in range(7)]
            added = [None] * width
            for block in range(chunk // 8):
                row = c * chunk + block * 8
                other = [spread[row : row + 8, k * S : (k + 1) * S] for k in range(SPREAD)]
                other += [
                    jnp.broadcast_to(listed[block * 8 : block * 8 + 8, 24 + k : 25 + k], (8, S))
                    for k in range(SPREAD, 7)
                ]
                r = [me[k] - other[k] for k in range(3)]
                u = [me[3 + k] - other[3 + k] for k in range(3)]
                squared = r[0] * r[0] + r[1] * r[1] + r[2] * r[2] + SOFTENING
                inverse = lax.rsqrt(squared)
                along = u[0] * r[0] + u[1] * r[1] + u[2] * r[2]
                overlap = jnp.maximum((me[6] + other[6]) * inverse - 1.0, 0.0)
                weight = overlap * (STIFFNESS - along * inverse)
                terms = [weight * r[k] for k in range(3)]
                if width == 9:
                    terms += [terms[left] * r[right] for left, right in PAIR_LIST]
                added = [
                    term if total is None else total + term for total, term in zip(added, terms)
                ]
            for k in range(width):
                row = (k * 8 + c) * 8
                sum_ref[row : row + 8, :] += added[k]
        return carry

    return one_step


def collected(width, sum_ref):
    out = []
    for k in range(width):
        parts = [sum_ref[pl.ds(k * 64 + sub, 8, stride=8), :] for sub in range(8)]
        while len(parts) > 1:
            parts = [parts[i] + parts[i + 1] for i in range(0, len(parts), 2)]
        out.append(parts[0])
    return jnp.concatenate(out, axis=0)


def contact_sums(cells, width, chunk, scratch, skip_own=False):
    local_ref, mine_ref, index_ref, base_ref, amount_ref, chosen_ref, list_ref, sum_ref = scratch
    count = len(cells)
    span = 16 if cells == OUTSIDE else count

    def first_row(a):
        return 8 if cells == OUTSIDE and a == 1 else 0

    def beside(a, b, z):
        return [
            n
            for n, (x, y, slot) in enumerate(cells)
            if abs(x - 1 - a) <= 1 and abs(y - 1 - b) <= 1 and abs(slot - z) <= 1
            and not (skip_own and (x, y, slot) == (a + 1, b + 1, z))
        ]

    sum_ref[...] = jnp.zeros((width * 64, S), F32)
    place = [local_ref[pl.ds(k, count, stride=8), :] for k in range(3)]
    radius = local_ref[pl.ds(6, count, stride=8), :]
    rows = row_ids((count, S))
    masks = []
    for c, (a, b, z) in enumerate(CELLS):
        mine = mine_ref[c * 8 : c * 8 + 8, :]
        live = mine[6:7] > 0.0
        low = jnp.min(jnp.where(live, mine, 1e9), axis=1, keepdims=True)
        high = jnp.max(jnp.where(live, mine, -1e9), axis=1, keepdims=True)
        part = slice(first_row(a), first_row(a) + span)
        reach = radius[part] + high[6:7]
        near = reach > 0.0
        inside = set(beside(a, b, z))
        for n in range(part.start, part.stop):
            if n not in inside:
                near = jnp.logical_and(near, rows[part] != n)
        for k in range(3):
            near = jnp.logical_and(near, place[k][part] + reach > low[k : k + 1])
            near = jnp.logical_and(near, place[k][part] - reach < high[k : k + 1])
        masks.append(jnp.where(near, 1.0, 0.0).astype(F32))
    mask = jnp.concatenate(masks, axis=0).astype(BF16)
    upper = one_hot(row_ids((S, 2 * S)) <= lane_ids((S, 2 * S)))
    sums = matmul(mask, upper)
    prefix, amount = sums[:, :S], sums[:, S:]
    before = one_hot(lane_ids((span, span)) < row_ids((span, span)))
    total = None
    for c in range(8):
        part = amount[c * span : (c + 1) * span]
        base = matmul(before, part.astype(BF16))
        base_ref[c * span : (c + 1) * span, :] = base.astype(jnp.int32)
        listed = base[span - 1 : span] + part[span - 1 : span]
        total = listed if total is None else jnp.maximum(total, listed)
    most = total.astype(jnp.int32)[0, 0]
    amount_ref[0 : 8 * span, :] = amount.astype(jnp.int32)
    wanted = lane_ids((8 * span, S)).astype(F32)
    index = jnp.zeros((8 * span, S), jnp.int32)
    for step in (64, 32, 16, 8, 4, 2, 1):
        probe = lane_gather(prefix, index + (step - 1))
        index = jnp.where(probe <= wanted, index + step, index)
    index_ref[0 : 8 * span, :] = index
    empty = jnp.where(row_ids((8, S)) == 6, DEAD, 0.0).astype(F32)

    def gather_tiles(t, carry):
        want = t * S + lane_ids((8 * span, S)) - base_ref[0 : 8 * span, :]
        valid = jnp.logical_and(want >= 0, want < amount_ref[0 : 8 * span, :])
        source = lane_gather(index_ref[0 : 8 * span, :], jnp.clip(want, 0, S - 1))
        chosen_ref[0 : 8 * span, :] = jnp.where(valid, source, -1)
        for c, (a, b, z) in enumerate(CELLS):
            tile = empty
            for n in beside(a, b, z):
                row = c * span + n - first_row(a)
                pick = jnp.broadcast_to(chosen_ref[row : row + 1, :], (8, S))
                values = lane_gather(local_ref[n * 8 : n * 8 + 8, :], jnp.maximum(pick, 0))
                tile = jnp.where(pick >= 0, values, tile)
            store_listed(list_ref, t, c, chunk, tile)
        return carry

    gather_tiles(0, 0)
    lax.fori_loop(1, (most + (S - 1)) // S, gather_tiles, 0)

    lax.fori_loop(
        0, (most + (chunk - 1)) // chunk, pair_step(width, chunk, mine_ref, list_ref, sum_ref), 0
    )
    return collected(width, sum_ref)


def own_sums(width, scratch):
    mine_ref, list_ref, sum_ref = scratch
    sum_ref[...] = jnp.zeros((width * 64, S), F32)
    for c in range(8):
        store_listed(list_ref, 0, c, 64, mine_ref[c * 8 : c * 8 + 8, :])
    step = pair_step(width, 64, mine_ref, list_ref, sum_ref)
    for part in range(2):
        step(part, 0)
    return collected(width, sum_ref)


def mass_of(radius):
    scaled = radius / RADIUS_REF
    return scaled * scaled * scaled


def fill_start(cells, read, own, depth, scratch):
    for n, (x, y, slot) in enumerate(cells):
        scratch[0][n * 8 : n * 8 + 8, :] = local_state(read(x, y, slot), centre_of(x, y, slot, depth))
    for c, (a, b, z) in enumerate(CELLS):
        scratch[1][c * 8 : c * 8 + 8, :] = local_state(
            own[c * 8 : c * 8 + 8, :], centre_of(a + 1, b + 1, z, depth)
        )


def place_state(ref, start, state):
    ref[start : start + 3, :] = state[0]
    ref[start + 3 : start + 6, :] = state[1]
    ref[start + 6 : start + 8, :] = state[2]


def fill_stepped(cells, read, speed, own, own_speed, depth, scratch):
    for n, (x, y, slot) in enumerate(cells):
        state = stepped_state(read(x, y, slot), speed(x, y, slot), centre_of(x, y, slot, depth))
        place_state(scratch[0], n * 8, state)
    for c, (a, b, z) in enumerate(CELLS):
        state = stepped_state(
            own[c * 8 : c * 8 + 8, :],
            own_speed[c * 4 : c * 4 + 4, :],
            centre_of(a + 1, b + 1, z, depth),
        )
        place_state(scratch[1], c * 8, state)


def step_inside(*refs):
    pieces, sums_out, scratch = refs[:-9], refs[-9], refs[-8:]
    fill_start(INSIDE, plane_reader(pieces, 8), pieces[0], lax.axis_index("depth"), scratch)
    sums_out[...] = contact_sums(INSIDE, 3, 64, scratch)


def step_outside(own, sums_in, far, near, own_out, inner_out, *scratch):
    fill_start(OUTSIDE, down_reader((far, near), 8), own, lax.axis_index("depth"), scratch)
    sums = sums_in[...] + contact_sums(OUTSIDE, 3, 32, scratch)
    radius = own[pl.ds(6, 8, stride=8), :]
    safe_mass = jnp.where(radius > 0.0, mass_of(radius), 1.0)
    for k in range(3):
        velocity = own[pl.ds(3 + k, 8, stride=8), :] + TIME_STEP * sums[k * 8 : k * 8 + 8] / safe_mass
        for c in range(8):
            own_out[c * 4 + k : c * 4 + k + 1, :] = velocity[c : c + 1]
    for c in range(8):
        own_out[c * 4 + 3 : c * 4 + 4, :] = jnp.zeros((1, S), F32)
    for column in range(4):
        inner_out[column * 4 : column * 4 + 4, :] = own_out[column * 8 + 4 : column * 8 + 8, :]


def field_own(
    grid, own, own_speed, coefficients, sums_out, high_out, low_out, chosen_out, model_out, *scratch
):
    model_out[...] = coefficients[...]
    depth = lax.axis_index("depth")
    down = lax.axis_index("down")
    cross = lax.axis_index("cross")
    rows = row_ids((64, S))
    near_x, near_y, near_z = rows // 16 - 1, (rows // 4) % 4 - 1, rows % 4 - 1
    centres = [index.astype(F32) - 0.5 for index in (near_x, near_y, near_z)]
    kernels = []
    for c, (a, b, z) in enumerate(CELLS):
        state = stepped_state(
            own[c * 8 : c * 8 + 8, :],
            own_speed[c * 4 : c * 4 + 4, :],
            centre_of(a + 1, b + 1, z, depth),
        )
        place = state[0]
        place_state(scratch[0], c * 8, state)
        squared = jnp.zeros((64, S), F32)
        for k in range(3):
            gap = place[k : k + 1] - centres[k]
            squared = squared + gap * gap
        kernel = jnp.exp(squared * (-0.5 / (KERNEL_WIDTH * KERNEL_WIDTH))) / KERNEL_NORM
        beside = jnp.logical_and(
            jnp.logical_and(jnp.abs(near_x - a) <= 1, jnp.abs(near_y - b) <= 1),
            jnp.abs(near_z - jnp.where(depth == z, 0, 1)) <= 1,
        )
        kernels.append(jnp.where(beside, kernel, 0.0))
    kernel_high, kernel_low = split(jnp.concatenate(kernels, axis=1))
    high_out[...] = kernel_high
    low_out[...] = kernel_low.astype(BF16)
    size_x, size_y, size_z = grid
    nodes = size_x * size_y * size_z
    lanes = lane_ids((64, nodes))
    row = row_ids((64, nodes))
    target_x = (down * 2 + row // 16 - 1 + size_x) % size_x
    target_y = (cross * 2 + (row // 4) % 4 - 1 + size_y) % size_y
    target_z = depth * 2 + row % 4 - 1
    inside = jnp.logical_and(target_z >= 0, target_z < size_z)
    target = (target_x * size_y + target_y) * size_z + target_z
    sums_out[...] = own_sums(9, scratch)
    chosen_out[...] = one_hot(jnp.logical_and(inside, lanes == target))


def field_inside(sums_in, *refs):
    split_at = (len(refs) - 9) // 2
    pieces, speeds, sums_out, scratch = refs[:split_at], refs[split_at:-9], refs[-9], refs[-8:]
    read, speed = plane_reader(pieces, 8), plane_reader(speeds, 4)
    fill_stepped(INSIDE, read, speed, pieces[0], speeds[0], lax.axis_index("depth"), scratch)
    sums_out[...] = sums_in[...] + contact_sums(INSIDE, 9, 64, scratch, True)


def field_outside(
    own, own_speed, sums_in, far_old, near_old, far_speed, near_speed, kernel_high, kernel_low, chosen,
    force_out, node_out, moment_ref, *scratch
):
    depth = lax.axis_index("depth")
    read, speed = down_reader((far_old, near_old), 8), down_reader((far_speed, near_speed), 4)
    fill_stepped(OUTSIDE, read, speed, own, own_speed, depth, scratch)
    sums = sums_in[...] + contact_sums(OUTSIDE, 9, 32, scratch)
    force_out[...] = sums[0:24]
    radius = own[pl.ds(6, 8, stride=8), :]
    mass = jnp.where(radius > 0.0, mass_of(radius), 0.0)
    moments = [mass] + [mass * own_speed[pl.ds(k, 8, stride=4), :] for k in range(3)]
    moments += [0.5 * sums[k * 8 : k * 8 + 8] for k in range(3, 9)]
    moment_ref[...] = jnp.zeros((16, 8 * S), F32)
    for m, moment in enumerate(moments):
        for c in range(8):
            moment_ref[m : m + 1, c * S : (c + 1) * S] = moment[c : c + 1]
    moment_high, moment_low = split(moment_ref[...])
    wide_part = matmul_turned(
        jnp.concatenate([moment_high, moment_low.astype(BF16)], axis=0), kernel_high[...]
    )
    near = wide_part[0:16] + wide_part[16:32] + matmul_turned(moment_high, kernel_low[...])
    near_high, rest = split(near)
    near_middle, near_low = split(rest)
    placed = matmul(
        jnp.concatenate([near_high, near_middle, near_low.astype(BF16)], axis=0), chosen[...]
    )
    node_out[...] = placed[0:16] + placed[16:32] + placed[32:48]


def library_kernel(
    grid, coefficients, mine, other, speed, force, velocity_out, force_out, residual_out, gram_out, moment_out, terms
):
    flat = lax.axis_index("depth") == 0
    for k in range(3):
        for a in range(2):
            for b in range(2):
                c = a * 4 + b * 2
                layers = [speed[(c + z) * 4 + k : (c + z) * 4 + k + 1, :] for z in range(2)]
                pulls = [force[k * 8 + c + z : k * 8 + c + z + 1, :] for z in range(2)]
                for z in range(2):
                    velocity_out[k, a, b, z : z + 1, :] = jnp.where(flat, layers[z], layers[1 - z])
                    force_out[k, a, b, z : z + 1, :] = jnp.where(flat, pulls[z], pulls[1 - z])
    fields = mine[...] + other[...]
    size_x, size_y, size_z = grid
    nodes = size_x * size_y * size_z
    lanes = lax.broadcasted_iota(jnp.int32, (1, nodes), 1)
    node_x = lanes // (size_y * size_z)
    node_y = (lanes // size_z) % size_y
    node_z = lanes % size_z
    rows = row_ids((8, nodes))
    density = fields[0:1]
    values = jnp.where(rows == 0, fields[0:8], fields[0:8] / (density + MASS_SHIFT))

    def moved(value, step):
        return pltpu.roll(value, step % nodes, 1)

    plane = size_y * size_z
    slope_x = (moved(values, -plane) - moved(values, plane)) * 0.5
    after_y = jnp.where(
        node_y == size_y - 1, moved(values, (size_y - 1) * size_z), moved(values, -size_z)
    )
    before_y = jnp.where(
        node_y == 0, moved(values, -(size_y - 1) * size_z), moved(values, size_z)
    )
    slope_y = (after_y - before_y) * 0.5
    after_z = jnp.where(node_z == size_z - 1, 0.0, moved(values, -1))
    before_z = jnp.where(node_z == 0, 0.0, moved(values, 1))
    slope_z = (after_z - before_z) * 0.5
    slopes = [[table[k : k + 1] for k in range(4)] for table in (slope_x, slope_y, slope_z)]
    strain = [
        [0.5 * (slopes[left][1 + right] + slopes[right][1 + left]) for right in range(3)]
        for left in range(3)
    ]
    divergence = strain[0][0] + strain[1][1] + strain[2][2]
    rate_sum = jnp.zeros_like(density)
    for left in range(3):
        for right in range(3):
            entry = strain[left][right]
            if left == right:
                entry = entry - divergence / 3.0
            rate_sum = rate_sum + entry * entry
    shear_rate = jnp.sqrt(2.0 * rate_sum + 0.01)
    stress = [fields[4 + k : 5 + k] for k in range(6)]
    pressure = (stress[0] + stress[3] + stress[5]) / 3.0
    deviator = (
        (stress[0] - pressure) ** 2
        + (stress[3] - pressure) ** 2
        + (stress[5] - pressure) ** 2
        + 2.0 * (stress[1] ** 2 + stress[2] ** 2 + stress[4] ** 2)
    )
    shear_stress = jnp.sqrt(0.5 * deviator + 0.01)
    pressure_scale = jnp.sqrt(pressure * pressure + 1.0)
    friction = shear_stress / pressure_scale
    features = [
        density,
        pressure / pressure_scale,
        shear_rate,
        shear_rate / jnp.sqrt(pressure_scale),
        divergence,
        slopes[0][0],
        slopes[1][0],
        slopes[2][0],
    ]
    entries = list(features)
    for left in range(8):
        for right in range(left, 8):
            entries.append(features[left] * features[right])
    for left in range(1, 5):
        entries.append(features[left] * features[left] * features[left])
    for k, entry in enumerate(entries):
        terms[k : k + 1, :] = entry
    table = terms[...]
    model = lax.dot_general(
        jnp.broadcast_to(coefficients[...], (8, TERMS)),
        table,
        (((1,), (0,)), ((), ())),
        precision=lax.Precision.HIGHEST,
        preferred_element_type=F32,
    )
    residual = friction - model[0:1]
    gram_out[...] = (
        lax.dot_general(
            table,
            table,
            (((1,), (1,)), ((), ())),
            precision=lax.Precision.HIGHEST,
            preferred_element_type=F32,
        )
        / nodes
    )
    moment = lax.dot_general(
        jnp.broadcast_to(friction, (8, nodes)),
        table,
        (((1,), (1,)), ((), ())),
        precision=lax.Precision.HIGHEST,
        preferred_element_type=F32,
    )
    moment_out[...] = moment[0:1] / nodes
    down = lax.axis_index("down")
    cross = lax.axis_index("cross")
    depth = lax.axis_index("depth")
    b_rows = lax.broadcasted_iota(jnp.int32, (2, 1), 0)
    z_lanes = lax.broadcasted_iota(jnp.int32, (2, 2), 1)
    for a in range(2):
        mine = jnp.logical_and(node_x == down * 2 + a, node_y == cross * 2 + b_rows)
        column = [
            jnp.sum(
                jnp.where(jnp.logical_and(mine, node_z == depth * 2 + z), residual, 0.0),
                axis=1,
                keepdims=True,
            )
            for z in range(2)
        ]
        residual_out[a] = jnp.where(z_lanes == 0, column[0], column[1])


def ring(axis, step):
    peers = lax.axis_size(axis)
    return [(i, (i + step) % peers) for i in range(peers)]


def exchange(own, inner, height, joined, beside=None):
    cross = lax.axis_size("cross")

    def cells(block, first, count):
        return block[first * height : (first + count) * height]

    if cross == 2 and not joined:
        side = lax.ppermute(own, "cross", [(0, 1), (1, 0)])
    depth_halo = lax.ppermute(inner, "depth", [(0, 1), (1, 0)])
    if cross == 2:
        if joined:
            side = lax.ppermute(
                jnp.concatenate([own, depth_halo], axis=0), "cross", [(0, 1), (1, 0)]
            )
            diag = cells(side, 8, 4)
            sides = [side]
        else:
            diag = lax.ppermute(inner, ("cross", "depth"), [(i, 3 - i) for i in range(4)])
            sides = [side, diag]

        def lateral(x):
            return [
                cells(side, x * 4 + 2, 2),
                cells(side, x * 4, 2),
                cells(diag, x * 2 + 1, 1),
                cells(diag, x * 2, 1),
            ]

    else:
        pairs = [(i * 2 + j, ((i + 1) % cross) * 2 + 1 - j) for i in range(cross) for j in range(2)]
        back = [(i * 2 + j, ((i - 1) % cross) * 2 + 1 - j) for i in range(cross) for j in range(2)]
        last = jnp.concatenate([cells(own, 2, 2), cells(own, 6, 2)], axis=0)
        first = jnp.concatenate([cells(own, 0, 2), cells(own, 4, 2)], axis=0)
        last_inner = jnp.concatenate([cells(inner, 1, 1), cells(inner, 3, 1)], axis=0)
        first_inner = jnp.concatenate([cells(inner, 0, 1), cells(inner, 2, 1)], axis=0)
        before = lax.ppermute(last, "cross", ring("cross", 1))
        after = lax.ppermute(first, "cross", ring("cross", -1))
        diag_before = lax.ppermute(last_inner, ("cross", "depth"), pairs)
        diag_after = lax.ppermute(first_inner, ("cross", "depth"), back)
        sides = [before, after, diag_before, diag_after]

        def lateral(x):
            return [
                cells(before, x * 2, 2),
                cells(after, x * 2, 2),
                cells(diag_before, x, 1),
                cells(diag_after, x, 1),
            ]

    def face(x):
        return jnp.concatenate([cells(own, x * 4, 4), cells(depth_halo, x * 2, 2)] + lateral(x), axis=0)

    downs = lax.axis_size("down")
    last, first = face(1), face(0)
    if beside is not None:
        mine, depth_halo = lax.optimization_barrier((own, depth_halo))
        last, first, result = lax.optimization_barrier((last, first, beside(mine)))
    if downs % 2 == 0:
        even = lax.rem(lax.axis_index("down"), 2) == 0
        near = [(i, i ^ 1) for i in range(downs)]
        far = [(i, (i - 1 + 2 * (i % 2)) % downs) for i in range(downs)]
        outside = [
            lax.ppermute(jnp.where(even, first, last), "down", far),
            lax.ppermute(jnp.where(even, last, first), "down", near),
        ]
    else:
        outside = [
            lax.ppermute(last, "down", ring("down", 1)),
            lax.ppermute(first, "down", ring("down", -1)),
        ]
    if beside is not None:
        return [own, depth_halo] + sides, outside, result
    return [own, depth_halo] + sides, outside


def shared(value, axes, peers):
    return [value] + [
        lax.ppermute(value, axes, [(i, i ^ k) for i in range(peers)]) for k in range(1, peers)
    ]


def tree_sum(parts):
    while len(parts) > 1:
        parts = [parts[k] + parts[k + 1] for k in range(0, len(parts), 2)]
    return parts[0]


def body(positions, velocities, sphere_radii, counts, coefficients):
    down, cross, depth = (lax.axis_size(name) for name in ("down", "cross", "depth"))
    grid = (2 * down, 2 * cross, 2 * depth)
    nodes = grid[0] * grid[1] * grid[2]
    params = pltpu.CompilerParams(vmem_limit_bytes=VMEM_LIMIT)
    vector_shape = jax.ShapeDtypeStruct((3, 2, 2, 2, S), F32)

    def rows(count):
        return jax.ShapeDtypeStruct((count, S), F32)

    def call(kernel, inputs, outputs, scratch, name, vectors=0):
        return pl.pallas_call(
            kernel,
            out_shape=outputs,
            in_specs=[VMEM_SPEC] * len(inputs),
            out_specs=jax.tree.map(lambda _: VMEM_SPEC, outputs),
            scratch_shapes=scratch,
            compiler_params=params,
            cost_estimate=pl.CostEstimate(flops=vectors, bytes_accessed=1 << 20, transcendentals=0),
            name=name,
        )(*inputs)

    own, inner = pl.pallas_call(
        pack_kernel,
        out_shape=(rows(64), rows(32)),
        in_specs=[pl.BlockSpec(memory_space=pl.ANY)] * 4,
        out_specs=(VMEM_SPEC, VMEM_SPEC),
        scratch_shapes=[
            pltpu.SMEM((2, 2, 2), jnp.int32),
            pltpu.VMEM((3, 2, 2, 2, S), F32),
            pltpu.VMEM((3, 2, 2, 2, S), F32),
            pltpu.VMEM((2, 2, 2, S), F32),
            pltpu.SemaphoreType.DMA((4,)),
        ],
        compiler_params=pltpu.CompilerParams(vmem_limit_bytes=60 * 1024 * 1024),
        name="pack",
    )(counts, positions, velocities, sphere_radii)
    inside, outside = exchange(own, inner, 8, True)
    sums = call(step_inside, inside, rows(24), contact_scratch(INSIDE, 3), "step_inside", 1 << 31)
    own_speed, inner_speed = call(
        step_outside, [own, sums] + outside, (rows(32), rows(16)), contact_scratch(OUTSIDE, 3), "step_outside", 1 << 30
    )
    table = jax.ShapeDtypeStruct((64, 8 * S), BF16)
    inside_speed, outside_speed, weights = exchange(
        own_speed,
        inner_speed,
        4,
        False,
        lambda speed: call(
            functools.partial(field_own, grid),
            [own, speed, coefficients.reshape(1, TERMS)],
            (
                rows(72),
                table,
                table,
                jax.ShapeDtypeStruct((64, nodes), BF16),
                jax.ShapeDtypeStruct((1, TERMS), F32),
            ),
            [
                pltpu.VMEM((8 * 8, S), F32),
                pltpu.VMEM((8 * S, 32), F32),
                pltpu.VMEM((9 * 8 * 8, S), F32),
            ],
            "field_own",
            1 << 30,
        ),
    )
    sums = call(
        field_inside, [weights[0]] + inside + inside_speed, rows(72), contact_scratch(INSIDE, 9), "field_inside", 1 << 31
    )
    force, partial = call(
        field_outside,
        [own, own_speed, sums] + outside + outside_speed + list(weights[1:4]),
        (rows(24), jax.ShapeDtypeStruct((16, nodes), F32)),
        [pltpu.VMEM((16, 8 * S), F32)] + contact_scratch(OUTSIDE, 9),
        "field_outside",
        1 << 30,
    )
    partial = tree_sum(shared(partial, ("cross", "depth"), cross * depth))
    distance = 1
    while distance < down:
        other = lax.ppermute(partial, "down", [(i, i ^ distance) for i in range(down)])
        distance = distance * 2
        if distance < down:
            partial = partial + other
    velocity_new, force_next, residual_field, gram_matrix, moment = pl.pallas_call(
        functools.partial(library_kernel, grid),
        out_shape=(
            vector_shape,
            vector_shape,
            jax.ShapeDtypeStruct((2, 2, 2), F32),
            jax.ShapeDtypeStruct((TERMS, TERMS), F32),
            jax.ShapeDtypeStruct((1, TERMS), F32),
        ),
        in_specs=[VMEM_SPEC] * 5,
        out_specs=(VMEM_SPEC,) * 5,
        scratch_shapes=[pltpu.VMEM((TERMS, nodes), F32)],
        compiler_params=params,
        name="library",
    )(weights[4], partial, other, own_speed, force)
    return (velocity_new, force_next, residual_field, gram_matrix, moment.reshape(TERMS))


def solution(mesh):
    return jax.shard_map(
        body,
        mesh=mesh,
        in_specs=(
            P(None, ("groups", "down"), "cross", "depth", None),
            P(None, ("groups", "down"), "cross", "depth", None),
            P(("groups", "down"), "cross", "depth", None),
            P(("groups", "down"), "cross", "depth"),
            P(),
        ),
        out_specs=(
            P(None, ("groups", "down"), "cross", "depth", None),
            P(None, ("groups", "down"), "cross", "depth", None),
            P(("groups", "down"), "cross", "depth"),
            P("groups", None),
            P("groups"),
        ),
        check_vma=False,
    )
```

profile of v0, /device:TPU:0, one launch (start us, length us, event | category | flops | bytes accessed | tf_op | source)
XLA Modules:
  0.0 45.3 jit_solution(15190284797324743104)
XLA Ops:
  0.6 1.4 %pack.1 = (f32[64,128]{1,0:T(8,128)}, f32[32,128]{1,0:T(8,128)}) custom-call(s32[2,2,2]{2,1,0:T(2,128)} %counts_hbm.1, f32[3,2,2,2,128]{4,3,2,1,0:T(2,128)} %positions_hbm.1, f32[3,2,2,2,128]{4,3,2,1,0:T(2,128)} %velocities_hbm.1, f32[2,2,2,128]{3,2,1,0:T(2,128)} %radii_hbm.1), custom_call_target="tpu_custom_call" | custom-call | tf_op jit(solution)/shard_map/pack/pallas_call | solution.py:709
  2.0 0.5 %collective-permute-start = (f32[32,128]{1,0:T(8,128)}, f32[32,128]{1,0:T(8,128)S(1)}, u32[]{:S(2)}, u32[]{:S(2)}) collective-permute-start(f32[32,128]{1,0:T(8,128)} %get-tuple-element.31), channel_id=1, source_target_pairs={{0,1},{1,0},{2,3},{3,2},{4,5},{5,4},{6,7},{7,6},{8,9},{9,8},{10,11... | collective-permute-start | bytes 49160 | tf_op jit(solution)/shard_map/ppermute | solution.py:608
  2.6 0.8 %constant_dynamic-update-slice_fusion.11 = (f32[96,128]{1,0:T(8,128)S(1)}, f32[96,128]{1,0:T(8,128)S(1)}) fusion(f32[64,128]{1,0:T(8,128)} %get-tuple-element.30.refs_0_.own), kind=kLoop, calls=%fused_computation.12 | loop fusion | bytes 65536
  3.4 0.3 collective-permute-done.refs_1_
  3.6 2.9 %collective-permute-start.1 = (f32[96,128]{1,0:T(8,128)S(1)}, f32[96,128]{1,0:T(8,128)S(1)}, u32[]{:S(2)}, u32[]{:S(2)}) collective-permute-start(f32[96,128]{1,0:T(8,128)S(1)} %pad_maximum_fusion), channel_id=1, source_target_pairs={{0,2},{2,0},{1,3},{3,1},{4,6},{6,4},{5,7},{7,5},{8,10},{10,8},{9,1... | collective-permute-start | bytes 147464 | tf_op jit(solution)/shard_map/ppermute | solution.py:611
  6.5 2.1 %collective-permute-done.1.refs_2_ = f32[96,128]{1,0:T(8,128)S(1)} collective-permute-done((f32[96,128]{1,0:T(8,128)S(1)}, f32[96,128]{1,0:T(8,128)S(1)}, u32[]{:S(2)}, u32[]{:S(2)}) %collective-permute-start.1) | collective-permute-done | bytes 49184 | tf_op jit(solution)/shard_map/ppermute | solution.py:611
  8.6 2.2 %collective-permute-start.3 = (f32[96,128]{1,0:T(8,128)S(1)}, f32[96,128]{1,0:T(8,128)S(1)}, u32[]{:S(2)}, u32[]{:S(2)}) collective-permute-start(f32[96,128]{1,0:T(8,128)S(1)} %get-tuple-element.55), channel_id=1, source_target_pairs={{0,4},{4,0},{8,12},{12,8},{1,5},{5,1},{9,13},{13,9},{2,6},{6,2},{1... | collective-permute-start | bytes 147464 | tf_op jit(solution)/shard_map/ppermute | solution.py:663
  10.8 2.5 %collective-permute-start.2 = (f32[96,128]{1,0:T(8,128)S(1)}, f32[96,128]{1,0:T(8,128)S(1)}, u32[]{:S(2)}, u32[]{:S(2)}) collective-permute-start(f32[96,128]{1,0:T(8,128)S(1)} %get-tuple-element.56), channel_id=1, source_target_pairs={{0,12},{4,8},{8,4},{12,0},{1,13},{5,9},{9,5},{13,1},{2,14},{6,10},... | collective-permute-start | bytes 147464 | tf_op jit(solution)/shard_map/ppermute | solution.py:662
  13.3 3.7 %step_inside.1.sums_in = f32[24,128]{1,0:T(8,128)S(1)} custom-call(f32[64,128]{1,0:T(8,128)S(1)} %copy-done, f32[32,128]{1,0:T(8,128)S(1)} %collective-permute-done.refs_1_, f32[96,128]{1,0:T(8,128)S(1)} %collective-permute-done.1.refs_2_), custom_call_target="tpu_custom_call" | custom-call | flops 2147483648 | bytes 1048576 | tf_op jit(solution)/shard_map/step_inside/pallas_call | solution.py:698
  17.0 0.0 collective-permute-done.2.far.far_old
  17.0 1.6 %step_outside.1 = (f32[32,128]{1,0:T(8,128)S(1)}, f32[16,128]{1,0:T(8,128)S(1)}) custom-call(f32[64,128]{1,0:T(8,128)S(1)} %copy-done, f32[24,128]{1,0:T(8,128)S(1)} %step_inside.1.sums_in, f32[96,128]{1,0:T(8,128)S(1)} %collective-permute-done.2.far.far_old, f32[96,128]{1,0:T(8,128)S(1)} %collective-permute-done.3.near.near_old), custom_call_target="tpu_custom_call" | custom-call | flops 1073741824 | bytes 1048576 | tf_op jit(solution)/shard_map/step_outside/pallas_call | solution.py:698
  18.6 0.1 collective-permute-start.6
  18.6 1.6 %collective-permute-start.4 = (f32[16,128]{1,0:T(8,128)S(1)}, f32[16,128]{1,0:T(8,128)S(1)}, u32[]{:S(2)}, u32[]{:S(2)}) collective-permute-start(f32[16,128]{1,0:T(8,128)S(1)} %get-tuple-element.33), channel_id=1, source_target_pairs={{0,1},{1,0},{2,3},{3,2},{4,5},{5,4},{6,7},{7,6},{8,9},{9,8},{10,11... | collective-permute-start | bytes 24584 | tf_op jit(solution)/shard_map/ppermute | solution.py:608
  20.3 0.5 %collective-permute-start.5 = (f32[32,128]{1,0:T(8,128)S(1)}, f32[32,128]{1,0:T(8,128)S(1)}, u32[]{:S(2)}, u32[]{:S(2)}) collective-permute-start(f32[32,128]{1,0:T(8,128)S(1)} %get-tuple-element.34.own_speed.refs_3_.speed), channel_id=1, source_target_pairs={{0,2},{2,0},{1,3},{3,1},{4,6},{6,4},{5,7},{7,5},{8,10},{10,8},{9,1... | collective-permute-start | bytes 49160 | tf_op jit(solution)/shard_map/ppermute | solution.py:607
  20.8 0.3 collective-permute-done.4.refs_4_
  21.1 0.7 %collective-permute-done.6.refs_6_ = f32[16,128]{1,0:T(8,128)S(1)} collective-permute-done((f32[16,128]{1,0:T(8,128)S(1)}, f32[16,128]{1,0:T(8,128)S(1)}, u32[]{:S(2)}, u32[]{:S(2)}) %collective-permute-start.6) | collective-permute-done | bytes 8224 | tf_op jit(solution)/shard_map/ppermute | solution.py:617
  21.7 0.7 %copy-done.1 = f32[48]{0:T(128)S(1)} copy-done((f32[48]{0:T(128)S(1)}, f32[48]{0:T(128)}, u32[]{:S(2)}) %copy-start.1) | copy-done | bytes 216
  22.4 1.4 %field_own.1 = (f32[72,128]{1,0:T(8,128)S(1)}, bf16[64,1024]{1,0:T(8,128)(2,1)S(1)}, bf16[64,1024]{1,0:T(8,128)(2,1)S(1)}, bf16[64,128]{1,0:T(8,128)(2,1)S(1)}, f32[1,48]{1,0:T(1,128)S(1)}) custom-call(f32[64,128]{1,0:T(8,128)S(1)} %copy-done, f32[32,128]{1,0:T(8,128)S(1)} %get-tuple-element.34.own_speed.refs_3_.speed, f32[1,48]{1,0:T(1,128)S(1)} %bitcast.2), custom_call_target="tpu_custom_call" | custom-call | flops 1073741824 | bytes 1048576 | tf_op jit(solution)/shard_map/field_own/pallas_call | solution.py:698
  23.8 0.2 collective-permute-done.5.refs_5_
  24.1 0.6 %collective-permute-start.8 = (f32[48,128]{1,0:T(8,128)S(1)}, f32[48,128]{1,0:T(8,128)S(1)}, u32[]{:S(2)}, u32[]{:S(2)}) collective-permute-start(f32[48,128]{1,0:T(8,128)S(1)} %get-tuple-element.57), channel_id=1, source_target_pairs={{0,4},{4,0},{8,12},{12,8},{1,5},{5,1},{9,13},{13,9},{2,6},{6,2},{1... | collective-permute-start | bytes 73736 | tf_op jit(solution)/shard_map/ppermute | solution.py:663
  24.6 2.1 %collective-permute-start.7 = (f32[48,128]{1,0:T(8,128)S(1)}, f32[48,128]{1,0:T(8,128)S(1)}, u32[]{:S(2)}, u32[]{:S(2)}) collective-permute-start(f32[48,128]{1,0:T(8,128)S(1)} %get-tuple-element.58), channel_id=1, source_target_pairs={{0,12},{4,8},{8,4},{12,0},{1,13},{5,9},{9,5},{13,1},{2,14},{6,10},... | collective-permute-start | bytes 73736 | tf_op jit(solution)/shard_map/ppermute | solution.py:662
  26.7 3.6 %field_inside.1.sums_in = f32[72,128]{1,0:T(8,128)S(1)} custom-call(f32[72,128]{1,0:T(8,128)S(1)} %get-tuple-element.41.sums_in, f32[64,128]{1,0:T(8,128)S(1)} %copy-done, f32[32,128]{1,0:T(8,128)S(1)} %collective-permute-done.refs_1_, f32[96,128]{1,0:T(8,128)S(1)} %collective-permute-done.1.refs_2_, ...), custom_call_target="tpu_custom_call" | custom-call | flops 2147483648 | bytes 1048576 | tf_op jit(solution)/shard_map/field_inside/pallas_call | solution.py:698
  30.4 2.0 %field_outside.1 = (f32[24,128]{1,0:T(8,128)S(1)}, f32[16,128]{1,0:T(8,128)S(1)}) custom-call(f32[64,128]{1,0:T(8,128)S(1)} %copy-done, f32[32,128]{1,0:T(8,128)S(1)} %get-tuple-element.34.own_speed.refs_3_.speed, f32[72,128]{1,0:T(8,128)S(1)} %field_inside.1.sums_in, f32[96,128]{1,0:T(8,128)S(1)} %collective-permute-done.2.far.far_old, ...), custom_call_target="tpu_custom_call" | custom-call | flops 1073741824 | bytes 1048576 | tf_op jit(solution)/shard_map/field_outside/pallas_call | solution.py:698
  32.4 1.7 %collective-permute-start.10 = (f32[16,128]{1,0:T(8,128)S(1)}, f32[16,128]{1,0:T(8,128)S(1)}, u32[]{:S(2)}, u32[]{:S(2)}) collective-permute-start(f32[16,128]{1,0:T(8,128)S(1)} %get-tuple-element.48), channel_id=1, source_target_pairs={{0,2},{1,3},{2,0},{3,1},{4,6},{5,7},{6,4},{7,5},{8,10},{9,11},{10,... | collective-permute-start | bytes 24584 | tf_op jit(solution)/shard_map/ppermute | solution.py:677
  34.0 0.2 collective-permute-start.9
  34.3 1.2 %collective-permute-done.11 = f32[16,128]{1,0:T(8,128)S(1)} collective-permute-done((f32[16,128]{1,0:T(8,128)S(1)}, f32[16,128]{1,0:T(8,128)S(1)}, u32[]{:S(2)}, u32[]{:S(2)}) %collective-permute-start.11) | collective-permute-done | bytes 8224 | tf_op jit(solution)/shard_map/ppermute | solution.py:677
  35.5 0.6 %collective-permute-done.10 = f32[16,128]{1,0:T(8,128)S(1)} collective-permute-done((f32[16,128]{1,0:T(8,128)S(1)}, f32[16,128]{1,0:T(8,128)S(1)}, u32[]{:S(2)}, u32[]{:S(2)}) %collective-permute-start.10) | collective-permute-done | bytes 8224 | tf_op jit(solution)/shard_map/ppermute | solution.py:677
  36.1 0.1 collective-permute-start.12
  36.2 3.6 %collective-permute-done.12 = f32[16,128]{1,0:T(8,128)S(1)} collective-permute-done((f32[16,128]{1,0:T(8,128)S(1)}, f32[16,128]{1,0:T(8,128)S(1)}, u32[]{:S(2)}, u32[]{:S(2)}) %collective-permute-start.12) | collective-permute-done | bytes 8224 | tf_op jit(solution)/shard_map/ppermute | solution.py:768
  39.8 0.9 %collective-permute-start.13 = (f32[16,128]{1,0:T(8,128)S(1)}, f32[16,128]{1,0:T(8,128)S(1)}, u32[]{:S(2)}, u32[]{:S(2)}) collective-permute-start(f32[16,128]{1,0:T(8,128)S(1)} %add.15.mine), channel_id=1, source_target_pairs={{0,8},{4,12},{8,0},{12,4},{1,9},{5,13},{9,1},{13,5},{2,10},{6,14},... | collective-permute-start | bytes 24584 | tf_op jit(solution)/shard_map/ppermute | solution.py:768
  40.7 3.7 %collective-permute-done.13.other = f32[16,128]{1,0:T(8,128)S(1)} collective-permute-done((f32[16,128]{1,0:T(8,128)S(1)}, f32[16,128]{1,0:T(8,128)S(1)}, u32[]{:S(2)}, u32[]{:S(2)}) %collective-permute-start.13) | collective-permute-done | bytes 8224 | tf_op jit(solution)/shard_map/ppermute | solution.py:768
  44.4 0.9 %library.1 = (f32[3,2,2,2,128]{4,3,2,1,0:T(2,128)}, f32[3,2,2,2,128]{4,3,2,1,0:T(2,128)}, f32[2,2,2]{2,1,0:T(2,128)}, f32[48,48]{1,0:T(8,128)}, f32[1,48]{1,0:T(1,128)}) custom-call(f32[1,48]{1,0:T(1,128)S(1)} %get-tuple-element.40.coefficients, f32[16,128]{1,0:T(8,128)S(1)} %add.15.mine, f32[16,128]{1,0:T(8,128)S(1)} %collective-permute-done.13.other, ...), custom_call_target="tpu_custom_call" | custom-call | tf_op jit(solution)/shard_map/library/pallas_call | solution.py:772
  (24 shorter events, 0.1 us)
Async XLA Ops:
  2.0 1.6 %collective-permute-start = (f32[32,128]{1,0:T(8,128)}, f32[32,128]{1,0:T(8,128)S(1)}, u32[]{:S(2)}, u32[]{:S(2)}) collective-permute-start(f32[32,128]{1,0:T(8,128)} %get-tuple-element.31), channel_id=1, source_target_pairs={{0,1},{1,0},{2,3},{3,2},{4,5},{5,4},{6,7},{7,6},{8,9},{9,8},{10,11... | collective-permute-start | bytes 49160 | tf_op jit(solution)/shard_map/ppermute | solution.py:608
  2.6 1.1 %copy-start = (f32[64,128]{1,0:T(8,128)S(1)}, f32[64,128]{1,0:T(8,128)}, u32[]{:S(2)}) copy-start(f32[64,128]{1,0:T(8,128)} %get-tuple-element.30.refs_0_.own) | copy-start | bytes 98308
  3.6 5.0 %collective-permute-start.1 = (f32[96,128]{1,0:T(8,128)S(1)}, f32[96,128]{1,0:T(8,128)S(1)}, u32[]{:S(2)}, u32[]{:S(2)}) collective-permute-start(f32[96,128]{1,0:T(8,128)S(1)} %pad_maximum_fusion), channel_id=1, source_target_pairs={{0,2},{2,0},{1,3},{3,1},{4,6},{6,4},{5,7},{7,5},{8,10},{10,8},{9,1... | collective-permute-start | bytes 147464 | tf_op jit(solution)/shard_map/ppermute | solution.py:611
  8.6 8.4 %collective-permute-start.3 = (f32[96,128]{1,0:T(8,128)S(1)}, f32[96,128]{1,0:T(8,128)S(1)}, u32[]{:S(2)}, u32[]{:S(2)}) collective-permute-start(f32[96,128]{1,0:T(8,128)S(1)} %get-tuple-element.55), channel_id=1, source_target_pairs={{0,4},{4,0},{8,12},{12,8},{1,5},{5,1},{9,13},{13,9},{2,6},{6,2},{1... | collective-permute-start | bytes 147464 | tf_op jit(solution)/shard_map/ppermute | solution.py:663
  10.8 6.2 %collective-permute-start.2 = (f32[96,128]{1,0:T(8,128)S(1)}, f32[96,128]{1,0:T(8,128)S(1)}, u32[]{:S(2)}, u32[]{:S(2)}) collective-permute-start(f32[96,128]{1,0:T(8,128)S(1)} %get-tuple-element.56), channel_id=1, source_target_pairs={{0,12},{4,8},{8,4},{12,0},{1,13},{5,9},{9,5},{13,1},{2,14},{6,10},... | collective-permute-start | bytes 147464 | tf_op jit(solution)/shard_map/ppermute | solution.py:662
  18.6 3.2 %collective-permute-start.6 = (f32[16,128]{1,0:T(8,128)S(1)}, f32[16,128]{1,0:T(8,128)S(1)}, u32[]{:S(2)}, u32[]{:S(2)}) collective-permute-start(f32[16,128]{1,0:T(8,128)S(1)} %get-tuple-element.33), channel_id=1, source_target_pairs={{0,3},{1,2},{2,1},{3,0},{4,7},{5,6},{6,5},{7,4},{8,11},{9,10},{10,... | collective-permute-start | bytes 24584 | tf_op jit(solution)/shard_map/ppermute | solution.py:617
  18.6 2.4 %collective-permute-start.4 = (f32[16,128]{1,0:T(8,128)S(1)}, f32[16,128]{1,0:T(8,128)S(1)}, u32[]{:S(2)}, u32[]{:S(2)}) collective-permute-start(f32[16,128]{1,0:T(8,128)S(1)} %get-tuple-element.33), channel_id=1, source_target_pairs={{0,1},{1,0},{2,3},{3,2},{4,5},{5,4},{6,7},{7,6},{8,9},{9,8},{10,11... | collective-permute-start | bytes 24584 | tf_op jit(solution)/shard_map/ppermute | solution.py:608
  20.3 3.7 %collective-permute-start.5 = (f32[32,128]{1,0:T(8,128)S(1)}, f32[32,128]{1,0:T(8,128)S(1)}, u32[]{:S(2)}, u32[]{:S(2)}) collective-permute-start(f32[32,128]{1,0:T(8,128)S(1)} %get-tuple-element.34.own_speed.refs_3_.speed), channel_id=1, source_target_pairs={{0,2},{2,0},{1,3},{3,1},{4,6},{6,4},{5,7},{7,5},{8,10},{10,8},{9,1... | collective-permute-start | bytes 49160 | tf_op jit(solution)/shard_map/ppermute | solution.py:607
  21.7 0.7 %copy-start.1 = (f32[48]{0:T(128)S(1)}, f32[48]{0:T(128)}, u32[]{:S(2)}) copy-start(f32[48]{0:T(128)} %param.9) | copy-start | bytes 580
  24.1 6.3 %collective-permute-start.8 = (f32[48,128]{1,0:T(8,128)S(1)}, f32[48,128]{1,0:T(8,128)S(1)}, u32[]{:S(2)}, u32[]{:S(2)}) collective-permute-start(f32[48,128]{1,0:T(8,128)S(1)} %get-tuple-element.57), channel_id=1, source_target_pairs={{0,4},{4,0},{8,12},{12,8},{1,5},{5,1},{9,13},{13,9},{2,6},{6,2},{1... | collective-permute-start | bytes 73736 | tf_op jit(solution)/shard_map/ppermute | solution.py:663
  24.6 5.8 %collective-permute-start.7 = (f32[48,128]{1,0:T(8,128)S(1)}, f32[48,128]{1,0:T(8,128)S(1)}, u32[]{:S(2)}, u32[]{:S(2)}) collective-permute-start(f32[48,128]{1,0:T(8,128)S(1)} %get-tuple-element.58), channel_id=1, source_target_pairs={{0,12},{4,8},{8,4},{12,0},{1,13},{5,9},{9,5},{13,1},{2,14},{6,10},... | collective-permute-start | bytes 73736 | tf_op jit(solution)/shard_map/ppermute | solution.py:662
  32.4 3.1 %collective-permute-start.11 = (f32[16,128]{1,0:T(8,128)S(1)}, f32[16,128]{1,0:T(8,128)S(1)}, u32[]{:S(2)}, u32[]{:S(2)}) collective-permute-start(f32[16,128]{1,0:T(8,128)S(1)} %get-tuple-element.48), channel_id=1, source_target_pairs={{0,3},{1,2},{2,1},{3,0},{4,7},{5,6},{6,5},{7,4},{8,11},{9,10},{10,... | collective-permute-start | bytes 24584 | tf_op jit(solution)/shard_map/ppermute | solution.py:677
  32.4 3.7 %collective-permute-start.10 = (f32[16,128]{1,0:T(8,128)S(1)}, f32[16,128]{1,0:T(8,128)S(1)}, u32[]{:S(2)}, u32[]{:S(2)}) collective-permute-start(f32[16,128]{1,0:T(8,128)S(1)} %get-tuple-element.48), channel_id=1, source_target_pairs={{0,2},{1,3},{2,0},{3,1},{4,6},{5,7},{6,4},{7,5},{8,10},{9,11},{10,... | collective-permute-start | bytes 24584 | tf_op jit(solution)/shard_map/ppermute | solution.py:677
  34.0 2.0 %collective-permute-start.9 = (f32[16,128]{1,0:T(8,128)S(1)}, f32[16,128]{1,0:T(8,128)S(1)}, u32[]{:S(2)}, u32[]{:S(2)}) collective-permute-start(f32[16,128]{1,0:T(8,128)S(1)} %get-tuple-element.48), channel_id=1, source_target_pairs={{0,1},{1,0},{2,3},{3,2},{4,5},{5,4},{6,7},{7,6},{8,9},{9,8},{10,11... | collective-permute-start | bytes 24584 | tf_op jit(solution)/shard_map/ppermute | solution.py:677
  36.1 3.7 %collective-permute-start.12 = (f32[16,128]{1,0:T(8,128)S(1)}, f32[16,128]{1,0:T(8,128)S(1)}, u32[]{:S(2)}, u32[]{:S(2)}) collective-permute-start(f32[16,128]{1,0:T(8,128)S(1)} %add_add_fusion), channel_id=1, source_target_pairs={{0,4},{4,0},{8,12},{12,8},{1,5},{5,1},{9,13},{13,9},{2,6},{6,2},{1... | collective-permute-start | bytes 24584 | tf_op jit(solution)/shard_map/ppermute | solution.py:768
  39.8 4.5 %collective-permute-start.13 = (f32[16,128]{1,0:T(8,128)S(1)}, f32[16,128]{1,0:T(8,128)S(1)}, u32[]{:S(2)}, u32[]{:S(2)}) collective-permute-start(f32[16,128]{1,0:T(8,128)S(1)} %add.15.mine), channel_id=1, source_target_pairs={{0,8},{4,12},{8,0},{12,4},{1,9},{5,13},{9,1},{13,5},{2,10},{6,14},... | collective-permute-start | bytes 24584 | tf_op jit(solution)/shard_map/ppermute | solution.py:768
where the time goes:
time: 45.4 us; the launch traced here: 45.3 us
  starting transfers between devices  15.8 us (35%)
  Pallas kernels  14.6 us (32%)
  waiting for transfers between devices  12.7 us (28%)
  local copies, waits for them, and re-layouts  1.52 us (3%)
  between operations  0.74 us (2%)
    pallas_call x5, Pallas kernels, call(): pl.pallas_call(kernel, out_shape=outputs, in_specs=[VMEM_SPEC] * len(inpu...  12.2 us
    ppermute x2, waiting for transfers between devices, body(): lax.ppermute(partial, 'down', [(i, i ^ distance) for i in range(down)])  7.31 us
    ppermute x2, starting transfers between devices, exchange(): lax.ppermute(jnp.where(even, first, last), 'down', far)  4.57 us
    ppermute x1, starting transfers between devices, exchange(): lax.ppermute(jnp.concatenate([own, depth_halo], axis=0), 'cross', [(0, 1)...  2.89 us
    ppermute x2, starting transfers between devices, exchange(): lax.ppermute(jnp.where(even, last, first), 'down', near)  2.75 us
    ppermute x2, starting transfers between devices, exchange(): depth_halo = lax.ppermute(inner, 'depth', [(0, 1), (1, 0)])  2.12 us
    ppermute x1, waiting for transfers between devices, exchange(): lax.ppermute(jnp.concatenate([own, depth_halo], axis=0), 'cross', [(0, 1)...  2.07 us
    ppermute x3, starting transfers between devices, shared(): lax.ppermute(value, axes, [(i, i ^ k) for i in range(peers)])  1.9 us
  transfers between devices with their start and end apart: 14, of which 9 were waited for; matrix products, arithmetic and copies ran while one was open for 2% of the time, Pallas kernels for 19%

commit v1 on v0

--- a/solution.py
+++ b/solution.py
@@ -383,9 +383,8 @@
 
 
 def field_own(
-    grid, own, own_speed, coefficients, sums_out, high_out, low_out, chosen_out, model_out, *scratch
+    grid, own, own_speed, sums_out, high_out, low_out, chosen_out, *scratch
 ):
-    model_out[...] = coefficients[...]
     depth = lax.axis_index("depth")
     down = lax.axis_index("down")
     cross = lax.axis_index("cross")
@@ -427,9 +426,11 @@
     chosen_out[...] = one_hot(jnp.logical_and(inside, lanes == target))
 
 
-def field_inside(sums_in, *refs):
-    split_at = (len(refs) - 9) // 2
-    pieces, speeds, sums_out, scratch = refs[:split_at], refs[split_at:-9], refs[-9], refs[-8:]
+def field_inside(sums_in, coefficients, *refs):
+    split_at = (len(refs) - 10) // 2
+    pieces, speeds, scratch = refs[:split_at], refs[split_at:-10], refs[-8:]
+    sums_out, model_out = refs[-10:-8]
+    model_out[...] = coefficients[...]
     read, speed = plane_reader(pieces, 8), plane_reader(speeds, 4)
     fill_stepped(INSIDE, read, speed, pieces[0], speeds[0], lax.axis_index("depth"), scratch)
     sums_out[...] = sums_in[...] + contact_sums(INSIDE, 9, 64, scratch, True)
@@ -465,9 +466,9 @@
     node_out[...] = placed[0:16] + placed[16:32] + placed[32:48]
 
 
-def library_kernel(
-    grid, coefficients, mine, other, speed, force, velocity_out, force_out, residual_out, gram_out, moment_out, terms
-):
+def library_kernel(grid, coefficients, *refs):
+    fields = tree_sum([ref[...] for ref in refs[:-8]])
+    speed, force, velocity_out, force_out, residual_out, gram_out, moment_out, terms = refs[-8:]
     flat = lax.axis_index("depth") == 0
     for k in range(3):
         for a in range(2):
@@ -478,7 +479,6 @@
                 for z in range(2):
                     velocity_out[k, a, b, z : z + 1, :] = jnp.where(flat, layers[z], layers[1 - z])
                     force_out[k, a, b, z : z + 1, :] = jnp.where(flat, pulls[z], pulls[1 - z])
-    fields = mine[...] + other[...]
     size_x, size_y, size_z = grid
     nodes = size_x * size_y * size_z
     lanes = lax.broadcasted_iota(jnp.int32, (1, nodes), 1)
@@ -672,10 +672,23 @@
     return [own, depth_halo] + sides, outside
 
 
-def shared(value, axes, peers):
-    return [value] + [
-        lax.ppermute(value, axes, [(i, i ^ k) for i in range(peers)]) for k in range(1, peers)
-    ]
+def summed_parts(value, fast, slow):
+    total = fast * slow
+    near = [1 << k for k in range(fast.bit_length() - 1)]
+    far = [fast << k for k in range(slow.bit_length() - 1)]
+    if 1 << (len(near) + len(far)) != total:
+        return [lax.psum(value, ("down", "cross", "depth"))]
+    parts = [value]
+    for k in range(max(len(near), len(far))):
+        value = tree_sum(parts)
+        masks = near[k : k + 1] + far[k : k + 1]
+        if len(masks) == 2:
+            masks.append(masks[0] ^ masks[1])
+        parts = [value] + [
+            lax.ppermute(value, ("down", "cross", "depth"), [(i, i ^ mask) for i in range(total)])
+            for mask in masks
+        ]
+    return parts
 
 
 def tree_sum(parts):
@@ -734,13 +747,12 @@
         False,
         lambda speed: call(
             functools.partial(field_own, grid),
-            [own, speed, coefficients.reshape(1, TERMS)],
+            [own, speed],
             (
                 rows(72),
                 table,
                 table,
                 jax.ShapeDtypeStruct((64, nodes), BF16),
-                jax.ShapeDtypeStruct((1, TERMS), F32),
             ),
             [
                 pltpu.VMEM((8 * 8, S), F32),
@@ -751,8 +763,13 @@
             1 << 30,
         ),
     )
-    sums = call(
-        field_inside, [weights[0]] + inside + inside_speed, rows(72), contact_scratch(INSIDE, 9), "field_inside", 1 << 31
+    sums, model = call(
+        field_inside,
+        [weights[0], coefficients.reshape(1, TERMS)] + inside + inside_speed,
+        (rows(72), jax.ShapeDtypeStruct((1, TERMS), F32)),
+        contact_scratch(INSIDE, 9),
+        "field_inside",
+        1 << 31,
     )
     force, partial = call(
         field_outside,
@@ -762,13 +779,7 @@
         "field_outside",
         1 << 30,
     )
-    partial = tree_sum(shared(partial, ("cross", "depth"), cross * depth))
-    distance = 1
-    while distance < down:
-        other = lax.ppermute(partial, "down", [(i, i ^ distance) for i in range(down)])
-        distance = distance * 2
-        if distance < down:
-            partial = partial + other
+    parts = summed_parts(partial, depth * cross, down)
     velocity_new, force_next, residual_field, gram_matrix, moment = pl.pallas_call(
         functools.partial(library_kernel, grid),
         out_shape=(
@@ -778,12 +789,12 @@
             jax.ShapeDtypeStruct((TERMS, TERMS), F32),
             jax.ShapeDtypeStruct((1, TERMS), F32),
         ),
-        in_specs=[VMEM_SPEC] * 5,
+        in_specs=[VMEM_SPEC] * (3 + len(parts)),
         out_specs=(VMEM_SPEC,) * 5,
         scratch_shapes=[pltpu.VMEM((TERMS, nodes), F32)],
         compiler_params=params,
         name="library",
-    )(weights[4], partial, other, own_speed, force)
+    )(model, *parts, own_speed, force)
     return (velocity_new, force_next, residual_field, gram_matrix, moment.reshape(TERMS))
 
 

time: 45.4 us -> 43.8 us (0.965)
  starting transfers between devices: 15.8 us -> 19.2 us
  waiting for transfers between devices: 12.7 us -> 9.76 us
  Pallas kernels: 14.6 us -> 13 us
  local copies, waits for them, and re-layouts: 1.52 us -> 0.87 us
    ppermute x5 -> x6, waiting for transfers between devices: 9.13 us -> 4.39 us  [summed_parts(): lax.ppermute(value, ('down', 'cross', 'depth'), [(i, i ^ mask) for i in r...]
    ppermute x5 -> x6, starting transfers between devices: 2.86 us -> 6.35 us  [summed_parts(): lax.ppermute(value, ('down', 'cross', 'depth'), [(i, i ^ mask) for i in r...]
    pallas_call x5, Pallas kernels: 12.2 us -> 10.7 us  [call(): pl.pallas_call(kernel, out_shape=outputs, in_specs=[VMEM_SPEC] * len(inpu...]
    ppermute x2, waiting for transfers between devices: 0.01 us -> 1.21 us  [exchange(): lax.ppermute(jnp.where(even, first, last), 'down', far)]
    unnamed x9, local copies, waits for them, and re-layouts: 1.46 us -> 0.81 us
    ppermute x1, waiting for transfers between devices: 0.23 us -> 0.86 us  [exchange(): side = lax.ppermute(own, 'cross', [(0, 1), (1, 0)])]
  transfers between devices with their start and end apart: 14 -> 15, of which waited for: 9 -> 12; matrix products, arithmetic and copies ran while one was open for 2% -> 2% of each run, Pallas kernels for 19% -> 16%
where the time goes in v1:
time: 43.8 us; the launch traced here: 43.6 us
  starting transfers between devices  19.2 us (44%)
  Pallas kernels  13 us (30%)
  waiting for transfers between devices  9.76 us (22%)
  local copies, waits for them, and re-layouts  0.87 us (2%)
  between operations  0.73 us (2%)
    pallas_call x5, Pallas kernels, call(): pl.pallas_call(kernel, out_shape=outputs, in_specs=[VMEM_SPEC] * len(inpu...  10.7 us
    ppermute x6, starting transfers between devices, summed_parts(): lax.ppermute(value, ('down', 'cross', 'depth'), [(i, i ^ mask) for i in r...  6.35 us
    ppermute x2, starting transfers between devices, exchange(): lax.ppermute(jnp.where(even, first, last), 'down', far)  4.45 us
    ppermute x6, waiting for transfers between devices, summed_parts(): lax.ppermute(value, ('down', 'cross', 'depth'), [(i, i ^ mask) for i in r...  4.39 us
    ppermute x1, starting transfers between devices, exchange(): lax.ppermute(jnp.concatenate([own, depth_halo], axis=0), 'cross', [(0, 1)...  2.89 us
    ppermute x2, starting transfers between devices, exchange(): lax.ppermute(jnp.where(even, last, first), 'down', near)  2.83 us
    ppermute x2, starting transfers between devices, exchange(): depth_halo = lax.ppermute(inner, 'depth', [(0, 1), (1, 0)])  2.11 us
    ppermute x1, waiting for transfers between devices, exchange(): lax.ppermute(jnp.concatenate([own, depth_halo], axis=0), 'cross', [(0, 1)...  2.07 us
  transfers between devices with their start and end apart: 15, of which 12 were waited for; matrix products, arithmetic and copies ran while one was open for 2% of the time, Pallas kernels for 16%

profile of v1, /device:TPU:0, one launch (start us, length us, event | category | flops | bytes accessed | tf_op | source)
XLA Modules:
  0.0 43.6 jit_solution(9610316266245959160)
XLA Ops:
  0.6 1.4 %pack.1 = (f32[64,128]{1,0:T(8,128)}, f32[32,128]{1,0:T(8,128)}) custom-call(s32[2,2,2]{2,1,0:T(2,128)} %counts_hbm.1, f32[3,2,2,2,128]{4,3,2,1,0:T(2,128)} %positions_hbm.1, f32[3,2,2,2,128]{4,3,2,1,0:T(2,128)} %velocities_hbm.1, f32[2,2,2,128]{3,2,1,0:T(2,128)} %radii_hbm.1), custom_call_target="tpu_custom_call" | custom-call | tf_op jit(solution)/shard_map/pack/pallas_call | solution.py:722
  2.0 0.5 %collective-permute-start = (f32[32,128]{1,0:T(8,128)}, f32[32,128]{1,0:T(8,128)S(1)}, u32[]{:S(2)}, u32[]{:S(2)}) collective-permute-start(f32[32,128]{1,0:T(8,128)} %get-tuple-element.31), channel_id=1, source_target_pairs={{0,1},{1,0},{2,3},{3,2},{4,5},{5,4},{6,7},{7,6},{8,9},{9,8},{10,11... | collective-permute-start | bytes 49160 | tf_op jit(solution)/shard_map/ppermute | solution.py:608
  2.6 0.8 %constant_dynamic-update-slice_fusion.11 = (f32[96,128]{1,0:T(8,128)S(1)}, f32[96,128]{1,0:T(8,128)S(1)}) fusion(f32[64,128]{1,0:T(8,128)} %get-tuple-element.30.refs_0_.own), kind=kLoop, calls=%fused_computation.12 | loop fusion | bytes 65536
  3.4 0.3 collective-permute-done.refs_1_
  3.6 2.9 %collective-permute-start.1 = (f32[96,128]{1,0:T(8,128)S(1)}, f32[96,128]{1,0:T(8,128)S(1)}, u32[]{:S(2)}, u32[]{:S(2)}) collective-permute-start(f32[96,128]{1,0:T(8,128)S(1)} %pad_maximum_fusion), channel_id=1, source_target_pairs={{0,2},{2,0},{1,3},{3,1},{4,6},{6,4},{5,7},{7,5},{8,10},{10,8},{9,1... | collective-permute-start | bytes 147464 | tf_op jit(solution)/shard_map/ppermute | solution.py:611
  6.5 2.1 %collective-permute-done.1.refs_2_ = f32[96,128]{1,0:T(8,128)S(1)} collective-permute-done((f32[96,128]{1,0:T(8,128)S(1)}, f32[96,128]{1,0:T(8,128)S(1)}, u32[]{:S(2)}, u32[]{:S(2)}) %collective-permute-start.1) | collective-permute-done | bytes 49184 | tf_op jit(solution)/shard_map/ppermute | solution.py:611
  8.6 2.2 %collective-permute-start.3 = (f32[96,128]{1,0:T(8,128)S(1)}, f32[96,128]{1,0:T(8,128)S(1)}, u32[]{:S(2)}, u32[]{:S(2)}) collective-permute-start(f32[96,128]{1,0:T(8,128)S(1)} %get-tuple-element.55), channel_id=1, source_target_pairs={{0,4},{4,0},{8,12},{12,8},{1,5},{5,1},{9,13},{13,9},{2,6},{6,2},{1... | collective-permute-start | bytes 147464 | tf_op jit(solution)/shard_map/ppermute | solution.py:663
  10.8 2.5 %collective-permute-start.2 = (f32[96,128]{1,0:T(8,128)S(1)}, f32[96,128]{1,0:T(8,128)S(1)}, u32[]{:S(2)}, u32[]{:S(2)}) collective-permute-start(f32[96,128]{1,0:T(8,128)S(1)} %get-tuple-element.56), channel_id=1, source_target_pairs={{0,12},{4,8},{8,4},{12,0},{1,13},{5,9},{9,5},{13,1},{2,14},{6,10},... | collective-permute-start | bytes 147464 | tf_op jit(solution)/shard_map/ppermute | solution.py:662
  13.3 3.3 %step_inside.1.sums_in = f32[24,128]{1,0:T(8,128)S(1)} custom-call(f32[64,128]{1,0:T(8,128)S(1)} %copy-done, f32[32,128]{1,0:T(8,128)S(1)} %collective-permute-done.refs_1_, f32[96,128]{1,0:T(8,128)S(1)} %collective-permute-done.1.refs_2_), custom_call_target="tpu_custom_call" | custom-call | flops 2147483648 | bytes 1048576 | tf_op jit(solution)/shard_map/step_inside/pallas_call | solution.py:711
  16.6 0.1 collective-permute-done.2.far.far_old
  16.7 1.5 %step_outside.1 = (f32[32,128]{1,0:T(8,128)S(1)}, f32[16,128]{1,0:T(8,128)S(1)}) custom-call(f32[64,128]{1,0:T(8,128)S(1)} %copy-done, f32[24,128]{1,0:T(8,128)S(1)} %step_inside.1.sums_in, f32[96,128]{1,0:T(8,128)S(1)} %collective-permute-done.2.far.far_old, f32[96,128]{1,0:T(8,128)S(1)} %collective-permute-done.3.near.near_old), custom_call_target="tpu_custom_call" | custom-call | flops 1073741824 | bytes 1048576 | tf_op jit(solution)/shard_map/step_outside/pallas_call | solution.py:711
  18.3 1.6 %collective-permute-start.4 = (f32[16,128]{1,0:T(8,128)S(1)}, f32[16,128]{1,0:T(8,128)S(1)}, u32[]{:S(2)}, u32[]{:S(2)}) collective-permute-start(f32[16,128]{1,0:T(8,128)S(1)} %get-tuple-element.33), channel_id=1, source_target_pairs={{0,1},{1,0},{2,3},{3,2},{4,5},{5,4},{6,7},{7,6},{8,9},{9,8},{10,11... | collective-permute-start | bytes 24584 | tf_op jit(solution)/shard_map/ppermute | solution.py:608
  19.9 0.5 %collective-permute-start.5 = (f32[32,128]{1,0:T(8,128)S(1)}, f32[32,128]{1,0:T(8,128)S(1)}, u32[]{:S(2)}, u32[]{:S(2)}) collective-permute-start(f32[32,128]{1,0:T(8,128)S(1)} %get-tuple-element.34.own_speed.refs_3_.refs_4_), channel_id=1, source_target_pairs={{0,2},{2,0},{1,3},{3,1},{4,6},{6,4},{5,7},{7,5},{8,10},{10,8},{9,1... | collective-permute-start | bytes 49160 | tf_op jit(solution)/shard_map/ppermute | solution.py:607
  20.4 0.3 collective-permute-done.4.refs_4_
  20.7 0.7 %collective-permute-done.6.refs_6_ = f32[16,128]{1,0:T(8,128)S(1)} collective-permute-done((f32[16,128]{1,0:T(8,128)S(1)}, f32[16,128]{1,0:T(8,128)S(1)}, u32[]{:S(2)}, u32[]{:S(2)}) %collective-permute-start.6) | collective-permute-done | bytes 8224 | tf_op jit(solution)/shard_map/ppermute | solution.py:617
  21.4 1.4 %field_own.1 = (f32[72,128]{1,0:T(8,128)S(1)}, bf16[64,1024]{1,0:T(8,128)(2,1)S(1)}, bf16[64,1024]{1,0:T(8,128)(2,1)S(1)}, bf16[64,128]{1,0:T(8,128)(2,1)S(1)}) custom-call(f32[64,128]{1,0:T(8,128)S(1)} %copy-done, f32[32,128]{1,0:T(8,128)S(1)} %get-tuple-element.34.own_speed.refs_3_.refs_4_), custom_call_target="tpu_custom_call" | custom-call | flops 1073741824 | bytes 1048576 | tf_op jit(solution)/shard_map/field_own/pallas_call | solution.py:711
  22.8 0.9 %collective-permute-done.5.refs_5_ = f32[32,128]{1,0:T(8,128)S(1)} collective-permute-done((f32[32,128]{1,0:T(8,128)S(1)}, f32[32,128]{1,0:T(8,128)S(1)}, u32[]{:S(2)}, u32[]{:S(2)}) %collective-permute-start.5) | collective-permute-done | bytes 16416 | tf_op jit(solution)/shard_map/ppermute | solution.py:607
  23.7 0.7 %collective-permute-start.8 = (f32[48,128]{1,0:T(8,128)S(1)}, f32[48,128]{1,0:T(8,128)S(1)}, u32[]{:S(2)}, u32[]{:S(2)}) collective-permute-start(f32[48,128]{1,0:T(8,128)S(1)} %get-tuple-element.57), channel_id=1, source_target_pairs={{0,4},{4,0},{8,12},{12,8},{1,5},{5,1},{9,13},{13,9},{2,6},{6,2},{1... | collective-permute-start | bytes 73736 | tf_op jit(solution)/shard_map/ppermute | solution.py:663
  24.4 2.0 %collective-permute-start.7 = (f32[48,128]{1,0:T(8,128)S(1)}, f32[48,128]{1,0:T(8,128)S(1)}, u32[]{:S(2)}, u32[]{:S(2)}) collective-permute-start(f32[48,128]{1,0:T(8,128)S(1)} %get-tuple-element.58), channel_id=1, source_target_pairs={{0,12},{4,8},{8,4},{12,0},{1,13},{5,9},{9,5},{13,1},{2,14},{6,10},... | collective-permute-start | bytes 73736 | tf_op jit(solution)/shard_map/ppermute | solution.py:662
  26.3 2.5 %field_inside.1 = (f32[72,128]{1,0:T(8,128)S(1)}, f32[1,48]{1,0:T(1,128)S(1)}) custom-call(f32[72,128]{1,0:T(8,128)S(1)} %get-tuple-element.39.sums_in, f32[1,48]{1,0:T(1,128)S(1)} %bitcast.2, f32[64,128]{1,0:T(8,128)S(1)} %copy-done, f32[32,128]{1,0:T(8,128)S(1)} %collective-permute-done.refs_1_, f32[96,128]{1,0:T(8,128)S(1)} %collective-permute-done.1.refs_2_, ...), custom_call_target="tpu_custom_call" | custom-call | flops 2147483648 | bytes 1048576 | tf_op jit(solution)/shard_map/field_inside/pallas_call | solution.py:711
  28.9 1.1 %collective-permute-done.7.far_speed = f32[48,128]{1,0:T(8,128)S(1)} collective-permute-done((f32[48,128]{1,0:T(8,128)S(1)}, f32[48,128]{1,0:T(8,128)S(1)}, u32[]{:S(2)}, u32[]{:S(2)}) %collective-permute-start.7) | collective-permute-done | bytes 24608 | tf_op jit(solution)/shard_map/ppermute | solution.py:662
  30.0 2.0 %field_outside.1 = (f32[24,128]{1,0:T(8,128)S(1)}, f32[16,128]{1,0:T(8,128)S(1)}) custom-call(f32[64,128]{1,0:T(8,128)S(1)} %copy-done, f32[32,128]{1,0:T(8,128)S(1)} %get-tuple-element.34.own_speed.refs_3_.refs_4_, f32[72,128]{1,0:T(8,128)S(1)} %get-tuple-element.42.sums_in, f32[96,128]{1,0:T(8,128)S(1)} %collective-permute-done.2.far.far_old, ...), custom_call_target="tpu_custom_call" | custom-call | flops 1073741824 | bytes 1048576 | tf_op jit(solution)/shard_map/field_outside/pallas_call | solution.py:711
  32.0 1.8 %collective-permute-start.9 = (f32[16,128]{1,0:T(8,128)S(1)}, f32[16,128]{1,0:T(8,128)S(1)}, u32[]{:S(2)}, u32[]{:S(2)}) collective-permute-start(f32[16,128]{1,0:T(8,128)S(1)} %get-tuple-element.48), channel_id=1, source_target_pairs={{0,1},{1,0},{2,3},{3,2},{4,5},{5,4},{6,7},{7,6},{8,9},{9,8},{10,11... | collective-permute-start | bytes 24584 | tf_op jit(solution)/shard_map/ppermute | solution.py:688
  33.8 1.2 %collective-permute-done.11 = f32[16,128]{1,0:T(8,128)S(1)} collective-permute-done((f32[16,128]{1,0:T(8,128)S(1)}, f32[16,128]{1,0:T(8,128)S(1)}, u32[]{:S(2)}, u32[]{:S(2)}) %collective-permute-start.11) | collective-permute-done | bytes 8224 | tf_op jit(solution)/shard_map/ppermute | solution.py:688
  35.1 0.6 %collective-permute-done.10 = f32[16,128]{1,0:T(8,128)S(1)} collective-permute-done((f32[16,128]{1,0:T(8,128)S(1)}, f32[16,128]{1,0:T(8,128)S(1)}, u32[]{:S(2)}, u32[]{:S(2)}) %collective-permute-start.10) | collective-permute-done | bytes 8224 | tf_op jit(solution)/shard_map/ppermute | solution.py:688
  35.7 1.1 %collective-permute-start.14 = (f32[16,128]{1,0:T(8,128)S(1)}, f32[16,128]{1,0:T(8,128)S(1)}, u32[]{:S(2)}, u32[]{:S(2)}) collective-permute-start(f32[16,128]{1,0:T(8,128)S(1)} %add_add_fusion.refs_0_), channel_id=1, source_target_pairs={{0,10},{1,11},{2,8},{3,9},{4,14},{5,15},{6,12},{7,13},{8,2},{9,3},... | collective-permute-start | bytes 24584 | tf_op jit(solution)/shard_map/ppermute | solution.py:688
  36.8 2.3 %collective-permute-start.13 = (f32[16,128]{1,0:T(8,128)S(1)}, f32[16,128]{1,0:T(8,128)S(1)}, u32[]{:S(2)}, u32[]{:S(2)}) collective-permute-start(f32[16,128]{1,0:T(8,128)S(1)} %add_add_fusion.refs_0_), channel_id=1, source_target_pairs={{0,8},{1,9},{2,10},{3,11},{4,12},{5,13},{6,14},{7,15},{8,0},{9,1},... | collective-permute-start | bytes 24584 | tf_op jit(solution)/shard_map/ppermute | solution.py:688
  39.1 1.1 %collective-permute-start.12 = (f32[16,128]{1,0:T(8,128)S(1)}, f32[16,128]{1,0:T(8,128)S(1)}, u32[]{:S(2)}, u32[]{:S(2)}) collective-permute-start(f32[16,128]{1,0:T(8,128)S(1)} %add_add_fusion.refs_0_), channel_id=1, source_target_pairs={{0,2},{1,3},{2,0},{3,1},{4,6},{5,7},{6,4},{7,5},{8,10},{9,11},{10,... | collective-permute-start | bytes 24584 | tf_op jit(solution)/shard_map/ppermute | solution.py:688
  40.1 1.1 %collective-permute-done.14.refs_3_ = f32[16,128]{1,0:T(8,128)S(1)} collective-permute-done((f32[16,128]{1,0:T(8,128)S(1)}, f32[16,128]{1,0:T(8,128)S(1)}, u32[]{:S(2)}, u32[]{:S(2)}) %collective-permute-start.14) | collective-permute-done | bytes 8224 | tf_op jit(solution)/shard_map/ppermute | solution.py:688
  41.2 0.1 collective-permute-done.13.refs_2_
  41.3 1.4 %collective-permute-done.12.refs_1_ = f32[16,128]{1,0:T(8,128)S(1)} collective-permute-done((f32[16,128]{1,0:T(8,128)S(1)}, f32[16,128]{1,0:T(8,128)S(1)}, u32[]{:S(2)}, u32[]{:S(2)}) %collective-permute-start.12) | collective-permute-done | bytes 8224 | tf_op jit(solution)/shard_map/ppermute | solution.py:688
  42.7 0.9 %library.1 = (f32[3,2,2,2,128]{4,3,2,1,0:T(2,128)}, f32[3,2,2,2,128]{4,3,2,1,0:T(2,128)}, f32[2,2,2]{2,1,0:T(2,128)}, f32[48,48]{1,0:T(8,128)}, f32[1,48]{1,0:T(1,128)}) custom-call(f32[1,48]{1,0:T(1,128)S(1)} %get-tuple-element.41.coefficients, f32[16,128]{1,0:T(8,128)S(1)} %add_add_fusion.refs_0_, f32[16,128]{1,0:T(8,128)S(1)} %collective-permute-done.12.refs_1_, ...), custom_call_target="tpu_custom_call" | custom-call | tf_op jit(solution)/shard_map/library/pallas_call | solution.py:783
  (25 shorter events, 0.3 us)
Async XLA Ops:
  2.0 1.6 %collective-permute-start = (f32[32,128]{1,0:T(8,128)}, f32[32,128]{1,0:T(8,128)S(1)}, u32[]{:S(2)}, u32[]{:S(2)}) collective-permute-start(f32[32,128]{1,0:T(8,128)} %get-tuple-element.31), channel_id=1, source_target_pairs={{0,1},{1,0},{2,3},{3,2},{4,5},{5,4},{6,7},{7,6},{8,9},{9,8},{10,11... | collective-permute-start | bytes 49160 | tf_op jit(solution)/shard_map/ppermute | solution.py:608
  2.6 1.1 %copy-start = (f32[64,128]{1,0:T(8,128)S(1)}, f32[64,128]{1,0:T(8,128)}, u32[]{:S(2)}) copy-start(f32[64,128]{1,0:T(8,128)} %get-tuple-element.30.refs_0_.own) | copy-start | bytes 98308
  3.6 5.0 %collective-permute-start.1 = (f32[96,128]{1,0:T(8,128)S(1)}, f32[96,128]{1,0:T(8,128)S(1)}, u32[]{:S(2)}, u32[]{:S(2)}) collective-permute-start(f32[96,128]{1,0:T(8,128)S(1)} %pad_maximum_fusion), channel_id=1, source_target_pairs={{0,2},{2,0},{1,3},{3,1},{4,6},{6,4},{5,7},{7,5},{8,10},{10,8},{9,1... | collective-permute-start | bytes 147464 | tf_op jit(solution)/shard_map/ppermute | solution.py:611
  8.6 7.9 %collective-permute-start.3 = (f32[96,128]{1,0:T(8,128)S(1)}, f32[96,128]{1,0:T(8,128)S(1)}, u32[]{:S(2)}, u32[]{:S(2)}) collective-permute-start(f32[96,128]{1,0:T(8,128)S(1)} %get-tuple-element.55), channel_id=1, source_target_pairs={{0,4},{4,0},{8,12},{12,8},{1,5},{5,1},{9,13},{13,9},{2,6},{6,2},{1... | collective-permute-start | bytes 147464 | tf_op jit(solution)/shard_map/ppermute | solution.py:663
  10.8 5.9 %collective-permute-start.2 = (f32[96,128]{1,0:T(8,128)S(1)}, f32[96,128]{1,0:T(8,128)S(1)}, u32[]{:S(2)}, u32[]{:S(2)}) collective-permute-start(f32[96,128]{1,0:T(8,128)S(1)} %get-tuple-element.56), channel_id=1, source_target_pairs={{0,12},{4,8},{8,4},{12,0},{1,13},{5,9},{9,5},{13,1},{2,14},{6,10},... | collective-permute-start | bytes 147464 | tf_op jit(solution)/shard_map/ppermute | solution.py:662
  18.2 3.2 %collective-permute-start.6 = (f32[16,128]{1,0:T(8,128)S(1)}, f32[16,128]{1,0:T(8,128)S(1)}, u32[]{:S(2)}, u32[]{:S(2)}) collective-permute-start(f32[16,128]{1,0:T(8,128)S(1)} %get-tuple-element.33), channel_id=1, source_target_pairs={{0,3},{1,2},{2,1},{3,0},{4,7},{5,6},{6,5},{7,4},{8,11},{9,10},{10,... | collective-permute-start | bytes 24584 | tf_op jit(solution)/shard_map/ppermute | solution.py:617
  18.3 2.4 %collective-permute-start.4 = (f32[16,128]{1,0:T(8,128)S(1)}, f32[16,128]{1,0:T(8,128)S(1)}, u32[]{:S(2)}, u32[]{:S(2)}) collective-permute-start(f32[16,128]{1,0:T(8,128)S(1)} %get-tuple-element.33), channel_id=1, source_target_pairs={{0,1},{1,0},{2,3},{3,2},{4,5},{5,4},{6,7},{7,6},{8,9},{9,8},{10,11... | collective-permute-start | bytes 24584 | tf_op jit(solution)/shard_map/ppermute | solution.py:608
  19.9 3.7 %collective-permute-start.5 = (f32[32,128]{1,0:T(8,128)S(1)}, f32[32,128]{1,0:T(8,128)S(1)}, u32[]{:S(2)}, u32[]{:S(2)}) collective-permute-start(f32[32,128]{1,0:T(8,128)S(1)} %get-tuple-element.34.own_speed.refs_3_.refs_4_), channel_id=1, source_target_pairs={{0,2},{2,0},{1,3},{3,1},{4,6},{6,4},{5,7},{7,5},{8,10},{10,8},{9,1... | collective-permute-start | bytes 49160 | tf_op jit(solution)/shard_map/ppermute | solution.py:607
  23.7 5.2 %collective-permute-start.8 = (f32[48,128]{1,0:T(8,128)S(1)}, f32[48,128]{1,0:T(8,128)S(1)}, u32[]{:S(2)}, u32[]{:S(2)}) collective-permute-start(f32[48,128]{1,0:T(8,128)S(1)} %get-tuple-element.57), channel_id=1, source_target_pairs={{0,4},{4,0},{8,12},{12,8},{1,5},{5,1},{9,13},{13,9},{2,6},{6,2},{1... | collective-permute-start | bytes 73736 | tf_op jit(solution)/shard_map/ppermute | solution.py:663
  24.4 2.0 %copy-start.1 = (f32[48]{0:T(128)S(1)}, f32[48]{0:T(128)}, u32[]{:S(2)}) copy-start(f32[48]{0:T(128)} %param.9) | copy-start | bytes 580
  24.4 5.6 %collective-permute-start.7 = (f32[48,128]{1,0:T(8,128)S(1)}, f32[48,128]{1,0:T(8,128)S(1)}, u32[]{:S(2)}, u32[]{:S(2)}) collective-permute-start(f32[48,128]{1,0:T(8,128)S(1)} %get-tuple-element.58), channel_id=1, source_target_pairs={{0,12},{4,8},{8,4},{12,0},{1,13},{5,9},{9,5},{13,1},{2,14},{6,10},... | collective-permute-start | bytes 73736 | tf_op jit(solution)/shard_map/ppermute | solution.py:662
  31.9 3.1 %collective-permute-start.11 = (f32[16,128]{1,0:T(8,128)S(1)}, f32[16,128]{1,0:T(8,128)S(1)}, u32[]{:S(2)}, u32[]{:S(2)}) collective-permute-start(f32[16,128]{1,0:T(8,128)S(1)} %get-tuple-element.48), channel_id=1, source_target_pairs={{0,5},{1,4},{2,7},{3,6},{4,1},{5,0},{6,3},{7,2},{8,13},{9,12},{10,... | collective-permute-start | bytes 24584 | tf_op jit(solution)/shard_map/ppermute | solution.py:688
  31.9 3.7 %collective-permute-start.10 = (f32[16,128]{1,0:T(8,128)S(1)}, f32[16,128]{1,0:T(8,128)S(1)}, u32[]{:S(2)}, u32[]{:S(2)}) collective-permute-start(f32[16,128]{1,0:T(8,128)S(1)} %get-tuple-element.48), channel_id=1, source_target_pairs={{0,4},{1,5},{2,6},{3,7},{4,0},{5,1},{6,2},{7,3},{8,12},{9,13},{10,... | collective-permute-start | bytes 24584 | tf_op jit(solution)/shard_map/ppermute | solution.py:688
  32.0 3.7 %collective-permute-start.9 = (f32[16,128]{1,0:T(8,128)S(1)}, f32[16,128]{1,0:T(8,128)S(1)}, u32[]{:S(2)}, u32[]{:S(2)}) collective-permute-start(f32[16,128]{1,0:T(8,128)S(1)} %get-tuple-element.48), channel_id=1, source_target_pairs={{0,1},{1,0},{2,3},{3,2},{4,5},{5,4},{6,7},{7,6},{8,9},{9,8},{10,11... | collective-permute-start | bytes 24584 | tf_op jit(solution)/shard_map/ppermute | solution.py:688
  35.7 5.5 %collective-permute-start.14 = (f32[16,128]{1,0:T(8,128)S(1)}, f32[16,128]{1,0:T(8,128)S(1)}, u32[]{:S(2)}, u32[]{:S(2)}) collective-permute-start(f32[16,128]{1,0:T(8,128)S(1)} %add_add_fusion.refs_0_), channel_id=1, source_target_pairs={{0,10},{1,11},{2,8},{3,9},{4,14},{5,15},{6,12},{7,13},{8,2},{9,3},... | collective-permute-start | bytes 24584 | tf_op jit(solution)/shard_map/ppermute | solution.py:688
  36.8 4.5 %collective-permute-start.13 = (f32[16,128]{1,0:T(8,128)S(1)}, f32[16,128]{1,0:T(8,128)S(1)}, u32[]{:S(2)}, u32[]{:S(2)}) collective-permute-start(f32[16,128]{1,0:T(8,128)S(1)} %add_add_fusion.refs_0_), channel_id=1, source_target_pairs={{0,8},{1,9},{2,10},{3,11},{4,12},{5,13},{6,14},{7,15},{8,0},{9,1},... | collective-permute-start | bytes 24584 | tf_op jit(solution)/shard_map/ppermute | solution.py:688
  39.1 3.7 %collective-permute-start.12 = (f32[16,128]{1,0:T(8,128)S(1)}, f32[16,128]{1,0:T(8,128)S(1)}, u32[]{:S(2)}, u32[]{:S(2)}) collective-permute-start(f32[16,128]{1,0:T(8,128)S(1)} %add_add_fusion.refs_0_), channel_id=1, source_target_pairs={{0,2},{1,3},{2,0},{3,1},{4,6},{5,7},{6,4},{7,5},{8,10},{9,11},{10,... | collective-permute-start | bytes 24584 | tf_op jit(solution)/shard_map/ppermute | solution.py:688
